TPU v7x, 32 devices: a whole 2x2x4 slice. The times are simulated.
32 devices in a mesh: section: 4 (over y, x), dp: 2 (over core), mp: 4 (over z).
Axes of the slice: x: 2, y: 2, z: 4, core: 2. Of those that a mesh axis runs over, the one named last changes fastest.
Arguments:
- cotangent: bfloat16 [256, 4096], P('dp', 'mp'), may hold values from -6 to 6
- saved_inputs: bfloat16 [4, 256, 4096], P('section', 'dp', 'mp'), may hold values from -6 to 6
- pre_acts: bfloat16 [4, 256, 4096], P('section', 'dp', 'mp'), may hold values from -8 to 8
- weights: bfloat16 [4, 4096, 4096], P('section', 'mp', 'dp'), may hold values from -0.046875 to 0.046875
- proj_in: bfloat16 [4, 4096, 64], P('section', 'mp'), may hold values from -0.09375 to 0.09375
- proj_out: bfloat16 [4, 4096, 64], P('section', 'mp'), may hold values from -0.09375 to 0.09375
- query_panels: float32 [4, 4, 4096], P('section', 'dp', 'mp'), may hold values from -4 to 4
- partners: int32 [2, 2], replicated, may hold values from 0 to 1, as said below
Outputs:
- train_panels: float32 [4, 8, 4096], P('section', 'dp', 'mp')
- scores: float32 [4, 2, 4], replicated
Inputs may be any that keep to these rules, and one draw needn't show every extreme that they name: The plan has 2 rounds: one round pairs every dp index with itself, and the others are the rounds of one round-robin plan of the 2 indices. The rows of partners hold each of these rounds once, in some order, so partners[r, partners[r, i]] = i.
All inputs are finite; a program needn't handle non-finite values.
Results may differ from a plain program's by a relative error of at most 0.02.
Values may be sent and summed in bfloat16 or wider, within the bound.
A program may use at most 64 MiB of HBM per device.

v0:
```python
import functools
import math

import jax
import jax.numpy as jnp
from jax import lax
from jax.experimental import pallas as pl
from jax.experimental.pallas import tpu as pltpu
from jax.sharding import PartitionSpec as P

LEN = 32
CHUNK = 16
W_PARTS = 4
MESH = pl.DeviceIdType.MESH


def ring(index, offset, count):
    return lax.rem(index + offset, count)


def dot_t(left, right):
    return lax.dot_general(
        left, right, (((1,), (1,)), ((), ())), preferred_element_type=jnp.float32
    )


def pack(block):
    half = block.shape[0] // 2
    return jnp.concatenate([block[:half], block[half:]], axis=1)


def unpack(block):
    half = block.shape[1] // 2
    return jnp.concatenate([block[:, :half], block[:, half:]], axis=0)


def relay_kernel(
    sizes, cot_hbm, inputs_hbm, pre_hbm, weights, proj_in_hbm, proj_out_hbm, queries_hbm, partners,
    panels, table,
    cot, inputs, pre, w_here, proj_in, proj_out, queries,
    g_own, g_all, d_in, d_out, sums_out, sums_in, slope, in_slots, out_slots, in_wide, q_all, p_tiled,
    layer_slots, section_slots, total, result,
    load, q_send, q_recv, g_send, g_recv, d_send, d_recv, s_send, s_recv,
    in_send, in_recv, out_send, out_recv, a_send, a_recv, b_send, b_recv, c_send, c_recv,
):
    n_sec, n_dp, n_mp = sizes
    sec = lax.axis_index("section")
    dp = lax.axis_index("dp")
    mp = lax.axis_index("mp")
    tokens, piece = cot.shape
    loads = [
        pltpu.make_async_copy(src, dst, load.at[at])
        for at, (src, dst) in enumerate((
            (pre_hbm.at[0], pre), (cot_hbm, cot), (inputs_hbm.at[0], inputs),
            (proj_in_hbm.at[0], proj_in), (queries_hbm.at[0], queries),
            (proj_out_hbm.at[0], proj_out), (weights.at[0], w_here),
        ))
    ]
    for copy in loads:
        copy.start()
    load_pre, load_cot, load_inputs, load_in, load_queries, load_out, load_w = loads
    chunks = tokens // CHUNK
    rank = proj_in.shape[0]
    examples = tokens // LEN
    piece_rank = rank // n_mp
    asked = queries.shape[0]
    rounds = partners.shape[0]
    w_cols = w_here.shape[1]
    w_rows = w_here.shape[0] // W_PARTS
    unit = min(piece, w_cols)
    top = n_sec - 1
    group = n_dp * n_mp
    here = dp * n_mp + mp

    barrier = pltpu.get_barrier_semaphore()
    for off in range(1, group):
        other = ring(here, off, group)
        pl.semaphore_signal(
            barrier, inc=1,
            device_id={"section": sec, "dp": other // n_mp, "mp": lax.rem(other, n_mp)},
            device_id_type=MESH,
        )
    for off in range(1, n_sec):
        pl.semaphore_signal(
            barrier, inc=1,
            device_id={"section": ring(sec, off, n_sec), "dp": dp, "mp": mp},
            device_id_type=MESH,
        )

    def to(section, dp_at, mp_at, src, dst, send_sem, recv_sem):
        return pltpu.make_async_remote_copy(
            src_ref=src, dst_ref=dst, send_sem=send_sem, recv_sem=recv_sem,
            device_id={"section": section, "dp": dp_at, "mp": mp_at}, device_id_type=MESH,
        )

    def q_copy(off):
        return to(sec, ring(dp, off, n_dp), mp, queries, q_all.at[dp],
                  q_send.at[off], q_recv.at[off])

    def g_target(sub):
        column = mp * piece + sub * unit
        return column // w_cols, lax.rem(column, w_cols) // unit

    def g_source(at):
        return (dp * w_cols + at * unit) // piece

    def g_spot(chunk, source_dp, at):
        return g_all.at[
            chunk, pl.ds(pl.multiple_of(source_dp * CHUNK, CHUNK), CHUNK),
            pl.ds(pl.multiple_of(at * unit, unit), unit),
        ]

    def g_copy(chunk, sub, off):
        rows = pl.ds(pl.multiple_of(chunk * CHUNK, CHUNK), CHUNK)
        target, at = g_target(sub)
        return to(sec, target, ring(mp, off, n_mp), g_own.at[rows, sub * unit:(sub + 1) * unit],
                  g_spot(chunk, dp, at), g_send.at[chunk, sub, off], g_recv.at[chunk, at, dp])

    def g_move(chunk, act):
        for sub in range(piece // unit):
            target, _ = g_target(sub)
            for off in range(1, n_mp):
                act(g_copy(chunk, sub, off))

            @pl.when(target != dp)
            def _():
                act(g_copy(chunk, sub, 0))

    def g_send_all(chunk):
        g_move(chunk, lambda copy: copy.start())
        rows = pl.ds(pl.multiple_of(chunk * CHUNK, CHUNK), CHUNK)
        for sub in range(piece // unit):
            target, at = g_target(sub)

            @pl.when(target == dp)
            def _():
                g_spot(chunk, dp, at)[...] = g_own[rows, sub * unit:(sub + 1) * unit]

    def g_wait(chunk):
        for at in range(w_cols // unit):
            source = g_source(at)
            for off in range(n_dp):
                source_dp = ring(dp, off, n_dp)

                def wait():
                    spot = g_spot(chunk, source_dp, at)
                    to(sec, dp, source, spot, spot, g_send.at[chunk, 0, 0],
                       g_recv.at[chunk, at, source_dp]).wait_recv()

                if off:
                    wait()
                else:
                    pl.when(source != mp)(wait)

    def s_copy(chunk, off):
        target = ring(dp, off, n_dp)
        return to(sec, target, mp,
                  sums_out.at[chunk, pl.ds(pl.multiple_of(target * CHUNK, CHUNK), CHUNK)],
                  sums_in.at[chunk, off], s_send.at[chunk, off], s_recv.at[chunk, off])

    def d_copy(chunk):
        rows = pl.ds(pl.multiple_of(chunk * CHUNK, CHUNK), CHUNK)
        return to(lax.rem(sec + n_sec - 1, n_sec), dp, mp, d_out.at[rows], d_in.at[rows],
                  d_send.at[chunk], d_recv.at[chunk])

    def side_copy(slots, off, send, recv):
        return to(sec, dp, ring(mp, off, n_mp), slots.at[0], slots.at[off],
                  send.at[off], recv.at[off])

    def a_copy():
        return to(0, dp, mp, total, layer_slots.at[sec], a_send, a_recv.at[sec])

    def b_copy(off):
        other = ring(here, off, group)
        return to(sec, other // n_mp, lax.rem(other, n_mp), section_slots.at[here],
                  section_slots.at[here], b_send.at[off], b_recv.at[off])

    def c_copy(section):
        return to(section, dp, mp, result, result, c_send.at[section], c_recv)

    load_pre.wait()
    slope_pre = pre[...].astype(jnp.float32)
    sigma = 1.0 / (1.0 + jnp.exp(-slope_pre))
    slope[...] = sigma * (1.0 + slope_pre * (1.0 - sigma))
    load_cot.wait()

    @pl.when(sec == top)
    def _():
        d_in[...] = cot[...]
        g_own[...] = (cot[...].astype(jnp.float32) * slope[...]).astype(jnp.bfloat16)

    pl.semaphore_wait(barrier, group - 1 + n_sec - 1)

    @pl.when(jnp.logical_and(sec == top, sec > 0))
    def _():
        @pl.loop(0, chunks)
        def _(chunk):
            g_send_all(chunk)

    load_queries.wait()
    q_all[dp] = queries[...]
    for off in range(1, n_dp):
        q_copy(off).start()

    load_inputs.wait()
    load_in.wait()
    in_slots[0] = pack(dot_t(inputs[...], proj_in[...]))
    for off in range(1, n_mp):
        side_copy(in_slots, off, in_send, in_recv).start()

    spread = (rank, piece_rank * rank)
    spread_row = lax.broadcasted_iota(jnp.int32, spread, 0)
    spread_col = lax.broadcasted_iota(jnp.int32, spread, 1)
    spread_in = (spread_row == mp * piece_rank + spread_col // rank).astype(jnp.bfloat16)
    spread_out = (spread_row == spread_col % rank).astype(jnp.bfloat16)

    for off in range(1, n_mp):
        side_copy(in_slots, off, in_send, in_recv).wait_recv()
    in_side = in_slots[0]
    for off in range(1, n_mp):
        in_side = in_side + in_slots[off]
    in_side = unpack(in_side) * (1.0 / math.sqrt(LEN))
    in_high = in_side.astype(jnp.bfloat16)
    in_low = (in_side - in_high.astype(jnp.float32)).astype(jnp.bfloat16)
    in_wide[...] = (
        jnp.dot(in_high, spread_in, preferred_element_type=jnp.float32)
        + jnp.dot(in_low, spread_in, preferred_element_type=jnp.float32)
    )

    q_row = lax.broadcasted_iota(jnp.int32, total.shape, 0)
    r_lane = lax.broadcasted_iota(jnp.int32, total.shape, 1)
    mask = jnp.zeros(total.shape, jnp.float32)
    for round_at in range(rounds):
        for index in range(n_dp):
            spot = jnp.logical_and(q_row // asked == index, r_lane // examples == round_at)
            hit = jnp.where(partners[round_at, index] == dp, 1.0, 0.0).astype(jnp.float32)
            mask = mask + jnp.where(spot, hit, 0.0)
    mask = mask * (1.0 / (rank * math.sqrt(n_sec)))
    p_tiled[...] = jnp.zeros_like(p_tiled)

    def step_rows(chunk):
        return pl.ds(pl.multiple_of(chunk * CHUNK, CHUNK), CHUNK)

    def take(chunk):
        rows = step_rows(chunk)
        d_copy(chunk).wait_recv()
        g_own[rows, :] = (d_in[rows, :].astype(jnp.float32) * slope[rows, :]).astype(jnp.bfloat16)

    def multiply(chunk):
        rows = step_rows(chunk)
        g_wait(chunk)
        for part in range(W_PARTS):
            cols = slice(part * w_rows, (part + 1) * w_rows)
            sums_out[chunk, :, cols] = dot_t(w_here[cols, :], g_all[chunk]).T
        for off in range(1, n_dp):
            s_copy(chunk, off).start()
        back = sums_out[chunk, pl.ds(pl.multiple_of(dp * CHUNK, CHUNK), CHUNK), :]
        for off in range(1, n_dp):
            s_copy(chunk, off).wait_recv()
            back = back + sums_in[chunk, off]
        d_out[rows, :] = (d_in[rows, :].astype(jnp.float32) + back).astype(jnp.bfloat16)
        d_copy(chunk).start()

    load_w.wait()
    load_out.wait()

    @pl.when(sec > 0)
    def _():
        @pl.loop(0, chunks + 1)
        def _(step):
            @pl.when(jnp.logical_and(sec < top, step < chunks))
            def _():
                take(step)
                g_send_all(step)

            @pl.when(step > 0)
            def _():
                multiply(step - 1)

    @pl.when(jnp.logical_and(sec == 0, sec < top))
    def _():
        @pl.loop(0, chunks)
        def _(step):
            take(step)

    out_slots[0] = pack(dot_t(g_own[...], proj_out[...])).astype(jnp.bfloat16)
    for off in range(1, n_mp):
        side_copy(out_slots, off, out_send, out_recv).start()
    for off in range(1, n_dp):
        q_copy(off).wait_recv()
    for off in range(1, n_mp):
        side_copy(out_slots, off, out_send, out_recv).wait_recv()
    out_side = out_slots[0].astype(jnp.float32)
    for off in range(1, n_mp):
        out_side = out_side + out_slots[off].astype(jnp.float32)
    out_wide = jnp.dot(
        unpack(out_side).astype(jnp.bfloat16), spread_out, preferred_element_type=jnp.float32
    )
    product = in_wide[...] * out_wide
    for example in range(examples):
        row = jnp.sum(product[example * LEN:(example + 1) * LEN], axis=0, keepdims=True)
        panels[0, example:example + 1, :] = row
        for round_at in range(rounds):
            at = round_at * examples + example
            p_tiled[at:at + 1, :] = row
    q_rows = [q_all[index] for index in range(n_dp)]
    pad = total.shape[0] - n_dp * asked
    if pad:
        q_rows.append(jnp.zeros((pad, q_all.shape[2]), jnp.float32))
    share = mask * lax.dot_general(
        jnp.concatenate(q_rows, axis=0), p_tiled[...], (((1,), (1,)), ((), ())),
        precision=lax.Precision.HIGHEST, preferred_element_type=jnp.float32,
    )

    @pl.when(sec > 0)
    def _():
        total[...] = share
        copy = a_copy()
        copy.start()
        copy.wait_send()
        c_copy(sec).wait_recv()

    @pl.when(sec == 0)
    def _():
        summed = share
        for section in range(1, n_sec):
            to(0, dp, mp, total, layer_slots.at[section], a_send, a_recv.at[section]).wait_recv()
            summed = summed + layer_slots[section]
        section_slots[here] = summed
        for off in range(1, group):
            b_copy(off).start()
        for off in range(1, group):
            b_copy(off).wait_recv()
        all_parts = section_slots[0]
        for slot in range(1, group):
            all_parts = all_parts + section_slots[slot]
        result[...] = all_parts
        for section in range(1, n_sec):
            c_copy(section).start()
        for off in range(1, group):
            b_copy(off).wait_send()
        for section in range(1, n_sec):
            c_copy(section).wait_send()

    table[...] = result[...]

    for off in range(1, n_dp):
        q_copy(off).wait_send()
    for off in range(1, n_mp):
        side_copy(in_slots, off, in_send, in_recv).wait_send()
        side_copy(out_slots, off, out_send, out_recv).wait_send()

    @pl.when(sec > 0)
    def _():
        @pl.loop(0, chunks)
        def _(chunk):
            g_move(chunk, lambda copy: copy.wait_send())
            for off in range(1, n_dp):
                s_copy(chunk, off).wait_send()
            d_copy(chunk).wait_send()


def body(sizes, cotangent, saved_inputs, pre_acts, weights, proj_in, proj_out, query_panels, partners):
    n_sec, n_dp, n_mp = sizes
    tokens, piece = cotangent.shape
    width = piece * n_mp
    w_cols = weights.shape[2]
    unit = min(piece, w_cols)
    rank = proj_in.shape[2]
    examples = tokens // LEN
    asked = query_panels.shape[1]
    rounds = partners.shape[0]
    chunks = tokens // CHUNK
    panel = query_panels.shape[2]
    q_rows = -(-(n_dp * asked) // 8) * 8
    lanes = 128
    group = n_dp * n_mp
    dma = pltpu.SemaphoreType.DMA
    vmem = pl.BlockSpec(memory_space=pltpu.VMEM)
    hbm = pl.BlockSpec(memory_space=pltpu.HBM)
    panels, table = pl.pallas_call(
        functools.partial(relay_kernel, sizes),
        out_shape=(
            jax.ShapeDtypeStruct((1, examples, panel), jnp.float32),
            jax.ShapeDtypeStruct((q_rows, lanes), jnp.float32),
        ),
        in_specs=[hbm] * 7 + [pl.BlockSpec(memory_space=pltpu.SMEM)],
        out_specs=(vmem, vmem),
        scratch_shapes=[
            pltpu.VMEM((tokens, piece), jnp.bfloat16),
            pltpu.VMEM((tokens, piece), jnp.bfloat16),
            pltpu.VMEM((tokens, piece), jnp.bfloat16),
            pltpu.VMEM((piece, w_cols), jnp.bfloat16),
            pltpu.VMEM((rank, piece), jnp.bfloat16),
            pltpu.VMEM((rank, piece), jnp.bfloat16),
            pltpu.VMEM((asked, panel), jnp.float32),
            pltpu.VMEM((tokens, piece), jnp.bfloat16),
            pltpu.VMEM((chunks, n_dp * CHUNK, w_cols), jnp.bfloat16),
            pltpu.VMEM((tokens, piece), jnp.bfloat16),
            pltpu.VMEM((tokens, piece), jnp.bfloat16),
            pltpu.VMEM((chunks, n_dp * CHUNK, piece), jnp.float32),
            pltpu.VMEM((chunks, n_dp, CHUNK, piece), jnp.float32),
            pltpu.VMEM((tokens, piece), jnp.float32),
            pltpu.VMEM((n_mp, tokens // 2, 2 * rank), jnp.float32),
            pltpu.VMEM((n_mp, tokens // 2, 2 * rank), jnp.bfloat16),
            pltpu.VMEM((tokens, panel), jnp.float32),
            pltpu.VMEM((n_dp, asked, panel), jnp.float32),
            pltpu.VMEM((lanes, panel), jnp.float32),
            pltpu.VMEM((n_sec, q_rows, lanes), jnp.float32),
            pltpu.VMEM((group, q_rows, lanes), jnp.float32),
            pltpu.VMEM((q_rows, lanes), jnp.float32),
            pltpu.VMEM((q_rows, lanes), jnp.float32),
            dma((7,)),
            dma((n_dp,)), dma((n_dp,)),
            dma((chunks, piece // unit, n_mp)), dma((chunks, w_cols // unit, n_dp)),
            dma((chunks,)), dma((chunks,)),
            dma((chunks, n_dp)), dma((chunks, n_dp)),
            dma((n_mp,)), dma((n_mp,)),
            dma((n_mp,)), dma((n_mp,)),
            dma, dma((n_sec,)),
            dma((group,)), dma((group,)),
            dma((n_sec,)), dma,
        ],
        compiler_params=pltpu.CompilerParams(
            collective_id=0, has_side_effects=True, vmem_limit_bytes=64 * 1024 * 1024
        ),
        cost_estimate=pl.CostEstimate(
            flops=2 * tokens * piece * width, bytes_accessed=2 * piece * w_cols, transcendentals=0
        ),
    )(cotangent, saved_inputs, pre_acts, weights, jnp.swapaxes(proj_in, 1, 2),
      jnp.swapaxes(proj_out, 1, 2), query_panels, partners)
    scores = table[: n_dp * asked, : rounds * examples].reshape(n_dp * asked, rounds, examples)
    return panels, scores


def solution(mesh):
    placed = (
        P("dp", "mp"),
        P("section", "dp", "mp"),
        P("section", "dp", "mp"),
        P("section", "mp", "dp"),
        P("section", "mp", None),
        P("section", "mp", None),
        P("section", "dp", "mp"),
        P(),
    )
    sizes = (mesh.shape["section"], mesh.shape["dp"], mesh.shape["mp"])
    return jax.shard_map(
        functools.partial(body, sizes), mesh=mesh, in_specs=placed,
        out_specs=(P("section", "dp", "mp"), P()), check_vma=False,
    )
```

profile of v0, /device:TPU:0, one launch (start us, length us, event | category | flops | bytes accessed | tf_op | source)
XLA Modules:
  0.0 96.1 jit_solution(13705369915950561779)
XLA Ops:
  0.6 92.8 %shard_map.95 = (f32[1,4,1024]{2,1,0:T(4,128)}, f32[8,128]{1,0:T(8,128)}) custom-call(bf16[128,1024]{1,0:T(8,128)(2,1)} %cot_hbm.1, bf16[1,128,1024]{2,1,0:T(8,128)(2,1)} %inputs_hbm.1, bf16[1,128,1024]{2,1,0:T(8,128)(2,1)} %pre_hbm.1, bf16[1,1024,2048]{2,1,0:T(8,128)(2,1)} %weights.1, bf16[1,64,1024]{2,1,0:T(8,128)(2,1)} %bitcast.2, ...), custom_call_target="tpu_custom_call" | custom-call | flops 1073741824 | bytes 4194304 | tf_op jit(solution)/shard_map/pallas_call | solution.py:381
  93.4 0.7 slice.3
  94.1 0.7 reshape.7
  94.8 1.3 %copy.11 = f32[1,4,1024]{2,1,0:T(4,128)} copy(f32[1,4,1024]{2,1,0:T(4,128)} %get-tuple-element.8) | data formatting | bytes 32768
where the time goes:
time: 96.4 us; the launch traced here: 96.1 us
  Pallas kernels  92.8 us (96%)
  local copies, waits for them, and re-layouts  2.67 us (3%)
    pallas_call x1, Pallas kernels, body(): pl.pallas_call(functools.partial(relay_kernel, sizes), out_shape=(jax.Sha...  92.8 us

commit v1 on v0

--- a/solution.py
+++ b/solution.py
@@ -191,12 +191,6 @@
 
     pl.semaphore_wait(barrier, group - 1 + n_sec - 1)
 
-    @pl.when(jnp.logical_and(sec == top, sec > 0))
-    def _():
-        @pl.loop(0, chunks)
-        def _(chunk):
-            g_send_all(chunk)
-
     load_queries.wait()
     q_all[dp] = queries[...]
     for off in range(1, n_dp):
@@ -268,9 +262,12 @@
     def _():
         @pl.loop(0, chunks + 1)
         def _(step):
-            @pl.when(jnp.logical_and(sec < top, step < chunks))
+            @pl.when(step < chunks)
             def _():
-                take(step)
+                @pl.when(sec < top)
+                def _():
+                    take(step)
+
                 g_send_all(step)
 
             @pl.when(step > 0)
@@ -342,7 +339,11 @@
         for section in range(1, n_sec):
             c_copy(section).wait_send()
 
-    table[...] = result[...]
+    for query in range(n_dp * asked):
+        for round_at in range(rounds):
+            table[query, round_at:round_at + 1, :] = result[
+                query:query + 1, round_at * examples:(round_at + 1) * examples
+            ]
 
     for off in range(1, n_dp):
         q_copy(off).wait_send()
@@ -378,11 +379,11 @@
     dma = pltpu.SemaphoreType.DMA
     vmem = pl.BlockSpec(memory_space=pltpu.VMEM)
     hbm = pl.BlockSpec(memory_space=pltpu.HBM)
-    panels, table = pl.pallas_call(
+    return pl.pallas_call(
         functools.partial(relay_kernel, sizes),
         out_shape=(
             jax.ShapeDtypeStruct((1, examples, panel), jnp.float32),
-            jax.ShapeDtypeStruct((q_rows, lanes), jnp.float32),
+            jax.ShapeDtypeStruct((n_dp * asked, rounds, examples), jnp.float32),
         ),
         in_specs=[hbm] * 7 + [pl.BlockSpec(memory_space=pltpu.SMEM)],
         out_specs=(vmem, vmem),
@@ -429,8 +430,6 @@
         ),
     )(cotangent, saved_inputs, pre_acts, weights, jnp.swapaxes(proj_in, 1, 2),
       jnp.swapaxes(proj_out, 1, 2), query_panels, partners)
-    scores = table[: n_dp * asked, : rounds * examples].reshape(n_dp * asked, rounds, examples)
-    return panels, scores
 
 
 def solution(mesh):

time: 96.4 us -> 80.3 us (0.83)
  Pallas kernels: 92.8 us -> 76.7 us
    pallas_call x1, Pallas kernels: 92.8 us -> 76.7 us  [body(): pl.pallas_call(functools.partial(relay_kernel, sizes), out_shape=(jax.Sha...]
    unnamed x1 -> x2, local copies, waits for them, and re-layouts: 1.32 us -> 2.59 us
where the time goes in v1:
time: 80.3 us; the launch traced here: 80 us
  Pallas kernels  76.7 us (96%)
  local copies, waits for them, and re-layouts  2.59 us (3%)
    pallas_call x1, Pallas kernels, body(): pl.pallas_call(functools.partial(relay_kernel, sizes), out_shape=(jax.Sha...  76.7 us
    unnamed x2, local copies, waits for them, and re-layouts  2.59 us

profile of v1, /device:TPU:0, one launch (start us, length us, event | category | flops | bytes accessed | tf_op | source)
XLA Modules:
  0.0 80.0 jit_solution(2172170477100895166)
XLA Ops:
  0.6 76.7 %shard_map.95 = (f32[1,4,1024]{2,1,0:T(4,128)}, f32[4,2,4]{2,1,0:T(2,128)}) custom-call(bf16[128,1024]{1,0:T(8,128)(2,1)} %cot_hbm.1, bf16[1,128,1024]{2,1,0:T(8,128)(2,1)} %inputs_hbm.1, bf16[1,128,1024]{2,1,0:T(8,128)(2,1)} %pre_hbm.1, bf16[1,1024,2048]{2,1,0:T(8,128)(2,1)} %weights.1, bf16[1,64,1024]{2,1,0:T(8,128)(2,1)} %bitcast.2, ...), custom_call_target="tpu_custom_call" | custom-call | flops 1073741824 | bytes 4194304 | tf_op jit(solution)/shard_map/pallas_call | solution.py:382
  77.4 1.3 %copy.12 = f32[1,4,1024]{2,1,0:T(4,128)} copy(f32[1,4,1024]{2,1,0:T(4,128)} %get-tuple-element.4) | data formatting | bytes 32768
  78.7 1.3 %copy.13 = f32[4,2,4]{2,1,0:T(2,128)} copy(f32[4,2,4]{2,1,0:T(2,128)} %get-tuple-element.5) | data formatting | bytes 256

commit v2 on v1

--- a/solution.py
+++ b/solution.py
@@ -9,7 +9,7 @@
 from jax.sharding import PartitionSpec as P
 
 LEN = 32
-CHUNK = 16
+CHUNK = 32
 W_PARTS = 4
 MESH = pl.DeviceIdType.MESH
 

time: 80.3 us -> 87.9 us (1.095)
  Pallas kernels: 76.7 us -> 84.4 us
    pallas_call x1, Pallas kernels: 76.7 us -> 84.4 us  [body(): pl.pallas_call(functools.partial(relay_kernel, sizes), out_shape=(jax.Sha...]
where the time goes in v2:
time: 87.9 us; the launch traced here: 87.6 us
  Pallas kernels  84.4 us (96%)
  local copies, waits for them, and re-layouts  2.59 us (3%)
    pallas_call x1, Pallas kernels, body(): pl.pallas_call(functools.partial(relay_kernel, sizes), out_shape=(jax.Sha...  84.4 us
    unnamed x2, local copies, waits for them, and re-layouts  2.59 us

profile of v2, /device:TPU:0, one launch (start us, length us, event | category | flops | bytes accessed | tf_op | source)
XLA Modules:
  0.0 87.6 jit_solution(2308499384058208978)
XLA Ops:
  0.6 84.4 %shard_map.95 = (f32[1,4,1024]{2,1,0:T(4,128)}, f32[4,2,4]{2,1,0:T(2,128)}) custom-call(bf16[128,1024]{1,0:T(8,128)(2,1)} %cot_hbm.1, bf16[1,128,1024]{2,1,0:T(8,128)(2,1)} %inputs_hbm.1, bf16[1,128,1024]{2,1,0:T(8,128)(2,1)} %pre_hbm.1, bf16[1,1024,2048]{2,1,0:T(8,128)(2,1)} %weights.1, bf16[1,64,1024]{2,1,0:T(8,128)(2,1)} %bitcast.2, ...), custom_call_target="tpu_custom_call" | custom-call | flops 1073741824 | bytes 4194304 | tf_op jit(solution)/shard_map/pallas_call | solution.py:382
  85.0 1.3 %copy.12 = f32[1,4,1024]{2,1,0:T(4,128)} copy(f32[1,4,1024]{2,1,0:T(4,128)} %get-tuple-element.4) | data formatting | bytes 32768
  86.3 1.3 %copy.13 = f32[4,2,4]{2,1,0:T(2,128)} copy(f32[4,2,4]{2,1,0:T(2,128)} %get-tuple-element.5) | data formatting | bytes 256

commit v3 on v1

--- a/solution.py
+++ b/solution.py
@@ -37,10 +37,10 @@
 def relay_kernel(
     sizes, cot_hbm, inputs_hbm, pre_hbm, weights, proj_in_hbm, proj_out_hbm, queries_hbm, partners,
     panels, table,
-    cot, inputs, pre, w_here, proj_in, proj_out, queries,
-    g_own, g_all, d_in, d_out, sums_out, sums_in, slope, in_slots, out_slots, in_wide, q_all, p_tiled,
+    cot, inputs, pre, w_here, proj_in, proj_wide, queries,
+    g_own, g_all, d_in, d_out, sums_out, sums_in, slope, in_slots, out_slots, in_wide, q_all, q_pad, spread_out, mask,
     layer_slots, section_slots, total, result,
-    load, q_send, q_recv, g_send, g_recv, d_send, d_recv, s_send, s_recv,
+    load, q_send, q_recv, g_send, g_recv, f_send, d_send, d_recv, s_send, s_recv,
     in_send, in_recv, out_send, out_recv, a_send, a_recv, b_send, b_recv, c_send, c_recv,
 ):
     n_sec, n_dp, n_mp = sizes
@@ -53,7 +53,7 @@
         for at, (src, dst) in enumerate((
             (pre_hbm.at[0], pre), (cot_hbm, cot), (inputs_hbm.at[0], inputs),
             (proj_in_hbm.at[0], proj_in), (queries_hbm.at[0], queries),
-            (proj_out_hbm.at[0], proj_out), (weights.at[0], w_here),
+            (proj_out_hbm.at[0], proj_wide.at[pl.ds(0, proj_out_hbm.shape[1])]), (weights.at[0], w_here),
         ))
     ]
     for copy in loads:
@@ -120,7 +120,12 @@
         for sub in range(piece // unit):
             target, _ = g_target(sub)
             for off in range(1, n_mp):
-                act(g_copy(chunk, sub, off))
+                if n_mp == 4 and off != 2:
+                    pl.when(mp != (0 if off == 3 else 3))(
+                        functools.partial(act, g_copy(chunk, sub, off))
+                    )
+                else:
+                    act(g_copy(chunk, sub, off))
 
             @pl.when(target != dp)
             def _():
@@ -136,21 +141,46 @@
             def _():
                 g_spot(chunk, dp, at)[...] = g_own[rows, sub * unit:(sub + 1) * unit]
 
+    def g_arrival(chunk, source_dp, at):
+        spot = g_spot(chunk, source_dp, at)
+        return to(sec, dp, mp, spot, spot, g_send.at[chunk, 0, 0], g_recv.at[chunk, at, source_dp])
+
+    def forwards(source):
+        return jnp.logical_or(
+            jnp.logical_and(source == 0, mp == 2), jnp.logical_and(source == 3, mp == 1)
+        )
+
+    def f_copy(chunk, source_dp, at):
+        spot = g_spot(chunk, source_dp, at)
+        return to(sec, dp, jnp.where(mp == 2, 3, 0), spot, spot,
+                  f_send.at[chunk, at, source_dp], g_recv.at[chunk, at, source_dp])
+
+    def forward(chunk, wait_send=False):
+        if n_mp != 4:
+            return
+        for at in range(w_cols // unit):
+            @pl.when(forwards(g_source(at)))
+            def _():
+                for off in range(n_dp):
+                    source_dp = ring(dp, off, n_dp)
+                    if wait_send:
+                        f_copy(chunk, source_dp, at).wait_send()
+                    else:
+                        g_arrival(chunk, source_dp, at).wait_recv()
+                        f_copy(chunk, source_dp, at).start()
+
     def g_wait(chunk):
         for at in range(w_cols // unit):
             source = g_source(at)
             for off in range(n_dp):
                 source_dp = ring(dp, off, n_dp)
-
-                def wait():
-                    spot = g_spot(chunk, source_dp, at)
-                    to(sec, dp, source, spot, spot, g_send.at[chunk, 0, 0],
-                       g_recv.at[chunk, at, source_dp]).wait_recv()
-
-                if off:
-                    wait()
-                else:
-                    pl.when(source != mp)(wait)
+                expected = source != mp if off == 0 else source >= 0
+                if n_mp == 4:
+                    expected = jnp.logical_and(expected, jnp.logical_not(forwards(source)))
+
+                @pl.when(expected)
+                def _():
+                    g_arrival(chunk, source_dp, at).wait_recv()
 
     def s_copy(chunk, off):
         target = ring(dp, off, n_dp)
@@ -163,9 +193,13 @@
         return to(lax.rem(sec + n_sec - 1, n_sec), dp, mp, d_out.at[rows], d_in.at[rows],
                   d_send.at[chunk], d_recv.at[chunk])
 
-    def side_copy(slots, off, send, recv):
-        return to(sec, dp, ring(mp, off, n_mp), slots.at[0], slots.at[off],
-                  send.at[off], recv.at[off])
+    def in_copy(off):
+        return to(sec, dp, ring(mp, off, n_mp), in_slots.at[0], in_slots.at[off],
+                  in_send.at[off], in_recv.at[off])
+
+    def out_copy(chunk, off):
+        return to(sec, dp, ring(mp, off, n_mp), out_slots.at[0, chunk], out_slots.at[off, chunk],
+                  out_send.at[chunk, off], out_recv.at[chunk, off])
 
     def a_copy():
         return to(0, dp, mp, total, layer_slots.at[sec], a_send, a_recv.at[sec])
@@ -191,46 +225,56 @@
 
     pl.semaphore_wait(barrier, group - 1 + n_sec - 1)
 
-    load_queries.wait()
-    q_all[dp] = queries[...]
-    for off in range(1, n_dp):
-        q_copy(off).start()
-
-    load_inputs.wait()
-    load_in.wait()
-    in_slots[0] = pack(dot_t(inputs[...], proj_in[...]))
-    for off in range(1, n_mp):
-        side_copy(in_slots, off, in_send, in_recv).start()
-
-    spread = (rank, piece_rank * rank)
-    spread_row = lax.broadcasted_iota(jnp.int32, spread, 0)
-    spread_col = lax.broadcasted_iota(jnp.int32, spread, 1)
-    spread_in = (spread_row == mp * piece_rank + spread_col // rank).astype(jnp.bfloat16)
-    spread_out = (spread_row == spread_col % rank).astype(jnp.bfloat16)
-
-    for off in range(1, n_mp):
-        side_copy(in_slots, off, in_send, in_recv).wait_recv()
-    in_side = in_slots[0]
-    for off in range(1, n_mp):
-        in_side = in_side + in_slots[off]
-    in_side = unpack(in_side) * (1.0 / math.sqrt(LEN))
-    in_high = in_side.astype(jnp.bfloat16)
-    in_low = (in_side - in_high.astype(jnp.float32)).astype(jnp.bfloat16)
-    in_wide[...] = (
-        jnp.dot(in_high, spread_in, preferred_element_type=jnp.float32)
-        + jnp.dot(in_low, spread_in, preferred_element_type=jnp.float32)
-    )
-
     q_row = lax.broadcasted_iota(jnp.int32, total.shape, 0)
     r_lane = lax.broadcasted_iota(jnp.int32, total.shape, 1)
-    mask = jnp.zeros(total.shape, jnp.float32)
-    for round_at in range(rounds):
+
+    def prepare():
+        load_queries.wait()
+        q_all[dp] = queries[...]
+        for off in range(1, n_dp):
+            q_copy(off).start()
+
+        load_inputs.wait()
+        load_in.wait()
+        in_slots[0] = pack(dot_t(inputs[...], proj_in[...]))
+        for off in range(1, n_mp):
+            in_copy(off).start()
+
+        spread = spread_out.shape
+        spread_row = lax.broadcasted_iota(jnp.int32, spread, 0)
+        spread_col = lax.broadcasted_iota(jnp.int32, spread, 1)
+        spread_out[...] = (spread_row == spread_col % rank).astype(jnp.bfloat16)
+        spread_in = (
+            spread_row[:rank] == mp * piece_rank + spread_col[:rank] // rank
+        ).astype(jnp.bfloat16)
+
+        chosen = jnp.zeros(total.shape, jnp.float32)
+        for round_at in range(rounds):
+            for index in range(n_dp):
+                spot = jnp.logical_and(q_row // asked == index, r_lane // examples == round_at)
+                hit = jnp.where(partners[round_at, index] == dp, 1.0, 0.0).astype(jnp.float32)
+                chosen = chosen + jnp.where(spot, hit, 0.0)
+        mask[...] = chosen * (1.0 / (rank * math.sqrt(n_sec)))
+        total[...] = jnp.zeros_like(total)
+
+        q_pad[...] = jnp.zeros_like(q_pad)
+        for off in range(1, n_dp):
+            q_copy(off).wait_recv()
         for index in range(n_dp):
-            spot = jnp.logical_and(q_row // asked == index, r_lane // examples == round_at)
-            hit = jnp.where(partners[round_at, index] == dp, 1.0, 0.0).astype(jnp.float32)
-            mask = mask + jnp.where(spot, hit, 0.0)
-    mask = mask * (1.0 / (rank * math.sqrt(n_sec)))
-    p_tiled[...] = jnp.zeros_like(p_tiled)
+            q_pad[index * asked:(index + 1) * asked, :] = q_all[index]
+
+        for off in range(1, n_mp):
+            in_copy(off).wait_recv()
+        in_side = in_slots[0]
+        for off in range(1, n_mp):
+            in_side = in_side + in_slots[off]
+        in_side = unpack(in_side) * (1.0 / math.sqrt(LEN))
+        in_high = in_side.astype(jnp.bfloat16)
+        in_low = (in_side - in_high.astype(jnp.float32)).astype(jnp.bfloat16)
+        in_wide[...] = (
+            jnp.dot(in_high, spread_in, preferred_element_type=jnp.float32)
+            + jnp.dot(in_low, spread_in, preferred_element_type=jnp.float32)
+        )
 
     def step_rows(chunk):
         return pl.ds(pl.multiple_of(chunk * CHUNK, CHUNK), CHUNK)
@@ -255,59 +299,78 @@
         d_out[rows, :] = (d_in[rows, :].astype(jnp.float32) + back).astype(jnp.bfloat16)
         d_copy(chunk).start()
 
+    def project(chunk):
+        out_slots[0, chunk] = dot_t(g_own[step_rows(chunk), :], proj_wide[...]).astype(jnp.bfloat16)
+        for off in range(1, n_mp):
+            out_copy(chunk, off).start()
+
+    per = LEN // CHUNK
+
+    def panel(example):
+        out_side = jnp.zeros((LEN, out_slots.shape[3]), jnp.float32)
+        for off in range(n_mp):
+            if off:
+                for at in range(per):
+                    out_copy(example * per + at, off).wait_recv()
+            block = out_slots[off, pl.ds(example * per, per)].astype(jnp.float32)
+            out_side = out_side + block.reshape(out_side.shape)
+        out_wide = jnp.dot(
+            out_side.astype(jnp.bfloat16), spread_out[...], preferred_element_type=jnp.float32
+        )
+        rows = pl.ds(pl.multiple_of(example * LEN, LEN), LEN)
+        row = jnp.sum(in_wide[rows, :] * out_wide, axis=0, keepdims=True)
+        panels[0, pl.ds(example, 1), :] = row
+        column = jnp.sum(q_pad[...] * row, axis=1, keepdims=True)
+        total[...] += jnp.where(lax.rem(r_lane, examples) == example, column, 0.0)
+
+    proj_wide[rank:, :] = jnp.zeros((proj_wide.shape[0] - rank, piece), jnp.bfloat16)
+    load_out.wait()
+    pl.when(sec < top)(prepare)
     load_w.wait()
-    load_out.wait()
 
     @pl.when(sec > 0)
     def _():
         @pl.loop(0, chunks + 1)
         def _(step):
-            @pl.when(step < chunks)
-            def _():
-                @pl.when(sec < top)
-                def _():
-                    take(step)
-
+            @pl.when(jnp.logical_and(sec == top, step < chunks))
+            def _():
                 g_send_all(step)
+                project(step)
 
             @pl.when(step > 0)
             def _():
+                forward(step - 1)
+
+            @pl.when(jnp.logical_and(sec < top, step < chunks))
+            def _():
+                take(step)
+                g_send_all(step)
+                project(step)
+
+            @pl.when(step > 0)
+            def _():
                 multiply(step - 1)
 
-    @pl.when(jnp.logical_and(sec == 0, sec < top))
+        pl.when(sec == top)(prepare)
+
+        @pl.loop(0, examples)
+        def _(example):
+            panel(example)
+
+    @pl.when(sec == 0)
     def _():
         @pl.loop(0, chunks)
         def _(step):
             take(step)
-
-    out_slots[0] = pack(dot_t(g_own[...], proj_out[...])).astype(jnp.bfloat16)
-    for off in range(1, n_mp):
-        side_copy(out_slots, off, out_send, out_recv).start()
-    for off in range(1, n_dp):
-        q_copy(off).wait_recv()
-    for off in range(1, n_mp):
-        side_copy(out_slots, off, out_send, out_recv).wait_recv()
-    out_side = out_slots[0].astype(jnp.float32)
-    for off in range(1, n_mp):
-        out_side = out_side + out_slots[off].astype(jnp.float32)
-    out_wide = jnp.dot(
-        unpack(out_side).astype(jnp.bfloat16), spread_out, preferred_element_type=jnp.float32
-    )
-    product = in_wide[...] * out_wide
-    for example in range(examples):
-        row = jnp.sum(product[example * LEN:(example + 1) * LEN], axis=0, keepdims=True)
-        panels[0, example:example + 1, :] = row
-        for round_at in range(rounds):
-            at = round_at * examples + example
-            p_tiled[at:at + 1, :] = row
-    q_rows = [q_all[index] for index in range(n_dp)]
-    pad = total.shape[0] - n_dp * asked
-    if pad:
-        q_rows.append(jnp.zeros((pad, q_all.shape[2]), jnp.float32))
-    share = mask * lax.dot_general(
-        jnp.concatenate(q_rows, axis=0), p_tiled[...], (((1,), (1,)), ((), ())),
-        precision=lax.Precision.HIGHEST, preferred_element_type=jnp.float32,
-    )
+            project(step)
+
+            @pl.when(jnp.logical_and(lax.rem(step, per) == per - 1, step >= 2 * per - 1))
+            def _():
+                panel(step // per - 1)
+
+        panel(examples - 1)
+
+    share = total[...] * mask[...]
 
     @pl.when(sec > 0)
     def _():
@@ -348,14 +411,19 @@
     for off in range(1, n_dp):
         q_copy(off).wait_send()
     for off in range(1, n_mp):
-        side_copy(in_slots, off, in_send, in_recv).wait_send()
-        side_copy(out_slots, off, out_send, out_recv).wait_send()
+        in_copy(off).wait_send()
+
+    @pl.loop(0, chunks)
+    def _(chunk):
+        for off in range(1, n_mp):
+            out_copy(chunk, off).wait_send()
 
     @pl.when(sec > 0)
     def _():
         @pl.loop(0, chunks)
         def _(chunk):
             g_move(chunk, lambda copy: copy.wait_send())
+            forward(chunk, wait_send=True)
             for off in range(1, n_dp):
                 s_copy(chunk, off).wait_send()
             d_copy(chunk).wait_send()
@@ -393,7 +461,7 @@
             pltpu.VMEM((tokens, piece), jnp.bfloat16),
             pltpu.VMEM((piece, w_cols), jnp.bfloat16),
             pltpu.VMEM((rank, piece), jnp.bfloat16),
-            pltpu.VMEM((rank, piece), jnp.bfloat16),
+            pltpu.VMEM((2 * rank, piece), jnp.bfloat16),
             pltpu.VMEM((asked, panel), jnp.float32),
             pltpu.VMEM((tokens, piece), jnp.bfloat16),
             pltpu.VMEM((chunks, n_dp * CHUNK, w_cols), jnp.bfloat16),
@@ -403,10 +471,12 @@
             pltpu.VMEM((chunks, n_dp, CHUNK, piece), jnp.float32),
             pltpu.VMEM((tokens, piece), jnp.float32),
             pltpu.VMEM((n_mp, tokens // 2, 2 * rank), jnp.float32),
-            pltpu.VMEM((n_mp, tokens // 2, 2 * rank), jnp.bfloat16),
+            pltpu.VMEM((n_mp, chunks, CHUNK, 2 * rank), jnp.bfloat16),
             pltpu.VMEM((tokens, panel), jnp.float32),
             pltpu.VMEM((n_dp, asked, panel), jnp.float32),
-            pltpu.VMEM((lanes, panel), jnp.float32),
+            pltpu.VMEM((q_rows, panel), jnp.float32),
+            pltpu.VMEM((2 * rank, panel), jnp.bfloat16),
+            pltpu.VMEM((q_rows, lanes), jnp.float32),
             pltpu.VMEM((n_sec, q_rows, lanes), jnp.float32),
             pltpu.VMEM((group, q_rows, lanes), jnp.float32),
             pltpu.VMEM((q_rows, lanes), jnp.float32),
@@ -414,10 +484,11 @@
             dma((7,)),
             dma((n_dp,)), dma((n_dp,)),
             dma((chunks, piece // unit, n_mp)), dma((chunks, w_cols // unit, n_dp)),
+            dma((chunks, w_cols // unit, n_dp)),
             dma((chunks,)), dma((chunks,)),
             dma((chunks, n_dp)), dma((chunks, n_dp)),
             dma((n_mp,)), dma((n_mp,)),
-            dma((n_mp,)), dma((n_mp,)),
+            dma((chunks, n_mp)), dma((chunks, n_mp)),
             dma, dma((n_sec,)),
             dma((group,)), dma((group,)),
             dma((n_sec,)), dma,

time: 80.3 us -> 88.5 us (1.10)
  Pallas kernels: 76.7 us -> 85 us
    pallas_call x1, Pallas kernels: 76.7 us -> 85 us  [body(): pl.pallas_call(functools.partial(relay_kernel, sizes), out_shape=(jax.Sha...]
where the time goes in v3:
time: 88.5 us; the launch traced here: 88.2 us
  Pallas kernels  85 us (96%)
  local copies, waits for them, and re-layouts  2.59 us (3%)
    pallas_call x1, Pallas kernels, body(): pl.pallas_call(functools.partial(relay_kernel, sizes), out_shape=(jax.Sha...  85 us
    unnamed x2, local copies, waits for them, and re-layouts  2.59 us

profile of v3, /device:TPU:0, one launch (start us, length us, event | category | flops | bytes accessed | tf_op | source)
XLA Modules:
  0.0 88.2 jit_solution(6701637932609714046)
XLA Ops:
  0.6 85.0 %shard_map.95 = (f32[1,4,1024]{2,1,0:T(4,128)}, f32[4,2,4]{2,1,0:T(2,128)}) custom-call(bf16[128,1024]{1,0:T(8,128)(2,1)} %cot_hbm.1, bf16[1,128,1024]{2,1,0:T(8,128)(2,1)} %inputs_hbm.1, bf16[1,128,1024]{2,1,0:T(8,128)(2,1)} %pre_hbm.1, bf16[1,1024,2048]{2,1,0:T(8,128)(2,1)} %weights.1, bf16[1,64,1024]{2,1,0:T(8,128)(2,1)} %bitcast.2, ...), custom_call_target="tpu_custom_call" | custom-call | flops 1073741824 | bytes 4194304 | tf_op jit(solution)/shard_map/pallas_call | solution.py:450
  85.6 1.3 %copy.12 = f32[1,4,1024]{2,1,0:T(4,128)} copy(f32[1,4,1024]{2,1,0:T(4,128)} %get-tuple-element.4) | data formatting | bytes 32768
  86.9 1.3 %copy.13 = f32[4,2,4]{2,1,0:T(2,128)} copy(f32[4,2,4]{2,1,0:T(2,128)} %get-tuple-element.5) | data formatting | bytes 256

commit v4 on v3

--- a/solution.py
+++ b/solution.py
@@ -40,7 +40,7 @@
     cot, inputs, pre, w_here, proj_in, proj_wide, queries,
     g_own, g_all, d_in, d_out, sums_out, sums_in, slope, in_slots, out_slots, in_wide, q_all, q_pad, spread_out, mask,
     layer_slots, section_slots, total, result,
-    load, q_send, q_recv, g_send, g_recv, f_send, d_send, d_recv, s_send, s_recv,
+    load, q_send, q_recv, g_send, g_recv, d_send, d_recv, s_send, s_recv,
     in_send, in_recv, out_send, out_recv, a_send, a_recv, b_send, b_recv, c_send, c_recv,
 ):
     n_sec, n_dp, n_mp = sizes
@@ -120,12 +120,7 @@
         for sub in range(piece // unit):
             target, _ = g_target(sub)
             for off in range(1, n_mp):
-                if n_mp == 4 and off != 2:
-                    pl.when(mp != (0 if off == 3 else 3))(
-                        functools.partial(act, g_copy(chunk, sub, off))
-                    )
-                else:
-                    act(g_copy(chunk, sub, off))
+                act(g_copy(chunk, sub, off))
 
             @pl.when(target != dp)
             def _():
@@ -145,42 +140,16 @@
         spot = g_spot(chunk, source_dp, at)
         return to(sec, dp, mp, spot, spot, g_send.at[chunk, 0, 0], g_recv.at[chunk, at, source_dp])
 
-    def forwards(source):
-        return jnp.logical_or(
-            jnp.logical_and(source == 0, mp == 2), jnp.logical_and(source == 3, mp == 1)
-        )
-
-    def f_copy(chunk, source_dp, at):
-        spot = g_spot(chunk, source_dp, at)
-        return to(sec, dp, jnp.where(mp == 2, 3, 0), spot, spot,
-                  f_send.at[chunk, at, source_dp], g_recv.at[chunk, at, source_dp])
-
-    def forward(chunk, wait_send=False):
-        if n_mp != 4:
-            return
-        for at in range(w_cols // unit):
-            @pl.when(forwards(g_source(at)))
-            def _():
-                for off in range(n_dp):
-                    source_dp = ring(dp, off, n_dp)
-                    if wait_send:
-                        f_copy(chunk, source_dp, at).wait_send()
-                    else:
-                        g_arrival(chunk, source_dp, at).wait_recv()
-                        f_copy(chunk, source_dp, at).start()
-
     def g_wait(chunk):
         for at in range(w_cols // unit):
             source = g_source(at)
             for off in range(n_dp):
                 source_dp = ring(dp, off, n_dp)
-                expected = source != mp if off == 0 else source >= 0
-                if n_mp == 4:
-                    expected = jnp.logical_and(expected, jnp.logical_not(forwards(source)))
-
-                @pl.when(expected)
-                def _():
-                    g_arrival(chunk, source_dp, at).wait_recv()
+                arrival = g_arrival(chunk, source_dp, at)
+                if off:
+                    arrival.wait_recv()
+                else:
+                    pl.when(source != mp)(arrival.wait_recv)
 
     def s_copy(chunk, off):
         target = ring(dp, off, n_dp)
@@ -197,9 +166,9 @@
         return to(sec, dp, ring(mp, off, n_mp), in_slots.at[0], in_slots.at[off],
                   in_send.at[off], in_recv.at[off])
 
-    def out_copy(chunk, off):
-        return to(sec, dp, ring(mp, off, n_mp), out_slots.at[0, chunk], out_slots.at[off, chunk],
-                  out_send.at[chunk, off], out_recv.at[chunk, off])
+    def out_copy(example, off):
+        return to(sec, dp, ring(mp, off, n_mp), out_slots.at[0, example], out_slots.at[off, example],
+                  out_send.at[example, off], out_recv.at[example, off])
 
     def a_copy():
         return to(0, dp, mp, total, layer_slots.at[sec], a_send, a_recv.at[sec])
@@ -299,10 +268,11 @@
         d_out[rows, :] = (d_in[rows, :].astype(jnp.float32) + back).astype(jnp.bfloat16)
         d_copy(chunk).start()
 
-    def project(chunk):
-        out_slots[0, chunk] = dot_t(g_own[step_rows(chunk), :], proj_wide[...]).astype(jnp.bfloat16)
+    def project(example):
+        rows = pl.ds(pl.multiple_of(example * LEN, LEN), LEN)
+        out_slots[0, example] = dot_t(g_own[rows, :], proj_wide[...]).astype(jnp.bfloat16)
         for off in range(1, n_mp):
-            out_copy(chunk, off).start()
+            out_copy(example, off).start()
 
     per = LEN // CHUNK
 
@@ -310,10 +280,8 @@
         out_side = jnp.zeros((LEN, out_slots.shape[3]), jnp.float32)
         for off in range(n_mp):
             if off:
-                for at in range(per):
-                    out_copy(example * per + at, off).wait_recv()
-            block = out_slots[off, pl.ds(example * per, per)].astype(jnp.float32)
-            out_side = out_side + block.reshape(out_side.shape)
+                out_copy(example, off).wait_recv()
+            out_side = out_side + out_slots[off, example].astype(jnp.float32)
         out_wide = jnp.dot(
             out_side.astype(jnp.bfloat16), spread_out[...], preferred_element_type=jnp.float32
         )
@@ -332,25 +300,22 @@
     def _():
         @pl.loop(0, chunks + 1)
         def _(step):
-            @pl.when(jnp.logical_and(sec == top, step < chunks))
+            @pl.when(step < chunks)
             def _():
+                @pl.when(sec < top)
+                def _():
+                    take(step)
+
                 g_send_all(step)
-                project(step)
-
-            @pl.when(step > 0)
-            def _():
-                forward(step - 1)
-
-            @pl.when(jnp.logical_and(sec < top, step < chunks))
-            def _():
-                take(step)
-                g_send_all(step)
-                project(step)
 
             @pl.when(step > 0)
             def _():
                 multiply(step - 1)
 
+                @pl.when(lax.rem(step, per) == 0)
+                def _():
+                    project(step // per - 1)
+
         pl.when(sec == top)(prepare)
 
         @pl.loop(0, examples)
@@ -362,11 +327,14 @@
         @pl.loop(0, chunks)
         def _(step):
             take(step)
-            project(step)
-
-            @pl.when(jnp.logical_and(lax.rem(step, per) == per - 1, step >= 2 * per - 1))
+
+            @pl.when(lax.rem(step, per) == per - 1)
             def _():
-                panel(step // per - 1)
+                project(step // per)
+
+                @pl.when(step >= per)
+                def _():
+                    panel(step // per - 1)
 
         panel(examples - 1)
 
@@ -413,17 +381,16 @@
     for off in range(1, n_mp):
         in_copy(off).wait_send()
 
-    @pl.loop(0, chunks)
-    def _(chunk):
+    @pl.loop(0, examples)
+    def _(example):
         for off in range(1, n_mp):
-            out_copy(chunk, off).wait_send()
+            out_copy(example, off).wait_send()
 
     @pl.when(sec > 0)
     def _():
         @pl.loop(0, chunks)
         def _(chunk):
             g_move(chunk, lambda copy: copy.wait_send())
-            forward(chunk, wait_send=True)
             for off in range(1, n_dp):
                 s_copy(chunk, off).wait_send()
             d_copy(chunk).wait_send()
@@ -471,7 +438,7 @@
             pltpu.VMEM((chunks, n_dp, CHUNK, piece), jnp.float32),
             pltpu.VMEM((tokens, piece), jnp.float32),
             pltpu.VMEM((n_mp, tokens // 2, 2 * rank), jnp.float32),
-            pltpu.VMEM((n_mp, chunks, CHUNK, 2 * rank), jnp.bfloat16),
+            pltpu.VMEM((n_mp, examples, LEN, 2 * rank), jnp.bfloat16),
             pltpu.VMEM((tokens, panel), jnp.float32),
             pltpu.VMEM((n_dp, asked, panel), jnp.float32),
             pltpu.VMEM((q_rows, panel), jnp.float32),
@@ -484,11 +451,10 @@
             dma((7,)),
             dma((n_dp,)), dma((n_dp,)),
             dma((chunks, piece // unit, n_mp)), dma((chunks, w_cols // unit, n_dp)),
-            dma((chunks, w_cols // unit, n_dp)),
             dma((chunks,)), dma((chunks,)),
             dma((chunks, n_dp)), dma((chunks, n_dp)),
             dma((n_mp,)), dma((n_mp,)),
-            dma((chunks, n_mp)), dma((chunks, n_mp)),
+            dma((examples, n_mp)), dma((examples, n_mp)),
             dma, dma((n_sec,)),
             dma((group,)), dma((group,)),
             dma((n_sec,)), dma,

time: 88.5 us -> 77.7 us (0.88)
  Pallas kernels: 85 us -> 74.2 us
    pallas_call x1, Pallas kernels: 85 us -> 74.2 us  [body(): pl.pallas_call(functools.partial(relay_kernel, sizes), out_shape=(jax.Sha...]
where the time goes in v4:
time: 77.7 us; the launch traced here: 77.4 us
  Pallas kernels  74.2 us (95%)
  local copies, waits for them, and re-layouts  2.59 us (3%)
    pallas_call x1, Pallas kernels, body(): pl.pallas_call(functools.partial(relay_kernel, sizes), out_shape=(jax.Sha...  74.2 us
    unnamed x2, local copies, waits for them, and re-layouts  2.59 us

profile of v4, /device:TPU:0, one launch (start us, length us, event | category | flops | bytes accessed | tf_op | source)
XLA Modules:
  0.0 77.4 jit_solution(10768689531747666845)
XLA Ops:
  0.6 74.2 %shard_map.95 = (f32[1,4,1024]{2,1,0:T(4,128)}, f32[4,2,4]{2,1,0:T(2,128)}) custom-call(bf16[128,1024]{1,0:T(8,128)(2,1)} %cot_hbm.1, bf16[1,128,1024]{2,1,0:T(8,128)(2,1)} %inputs_hbm.1, bf16[1,128,1024]{2,1,0:T(8,128)(2,1)} %pre_hbm.1, bf16[1,1024,2048]{2,1,0:T(8,128)(2,1)} %weights.1, bf16[1,64,1024]{2,1,0:T(8,128)(2,1)} %bitcast.2, ...), custom_call_target="tpu_custom_call" | custom-call | flops 1073741824 | bytes 4194304 | tf_op jit(solution)/shard_map/pallas_call | solution.py:417
  74.8 1.3 %copy.12 = f32[1,4,1024]{2,1,0:T(4,128)} copy(f32[1,4,1024]{2,1,0:T(4,128)} %get-tuple-element.4) | data formatting | bytes 32768
  76.1 1.3 %copy.13 = f32[4,2,4]{2,1,0:T(2,128)} copy(f32[4,2,4]{2,1,0:T(2,128)} %get-tuple-element.5) | data formatting | bytes 256

commit v5 on v4

--- a/solution.py
+++ b/solution.py
@@ -38,9 +38,9 @@
     sizes, cot_hbm, inputs_hbm, pre_hbm, weights, proj_in_hbm, proj_out_hbm, queries_hbm, partners,
     panels, table,
     cot, inputs, pre, w_here, proj_in, proj_wide, queries,
-    g_own, g_all, d_in, d_out, sums_out, sums_in, slope, in_slots, out_slots, in_wide, q_all, q_pad, spread_out, mask,
+    g_own, g_all, d_own, d_in, d_out, slope, in_slots, out_slots, in_wide, q_all, q_pad, spread_out, mask,
     layer_slots, section_slots, total, result,
-    load, q_send, q_recv, g_send, g_recv, d_send, d_recv, s_send, s_recv,
+    load, q_send, q_recv, g_send, g_recv, d_send, d_recv,
     in_send, in_recv, out_send, out_recv, a_send, a_recv, b_send, b_recv, c_send, c_recv,
 ):
     n_sec, n_dp, n_mp = sizes
@@ -86,6 +86,15 @@
             device_id={"section": ring(sec, off, n_sec), "dp": dp, "mp": mp},
             device_id_type=MESH,
         )
+    for step in (1, n_sec - 1):
+        for off in range(1, n_dp):
+            pl.semaphore_signal(
+                barrier, inc=1,
+                device_id={
+                    "section": ring(sec, step, n_sec), "dp": ring(dp, off, n_dp), "mp": mp
+                },
+                device_id_type=MESH,
+            )
 
     def to(section, dp_at, mp_at, src, dst, send_sem, recv_sem):
         return pltpu.make_async_remote_copy(
@@ -151,16 +160,16 @@
                 else:
                     pl.when(source != mp)(arrival.wait_recv)
 
-    def s_copy(chunk, off):
-        target = ring(dp, off, n_dp)
-        return to(sec, target, mp,
-                  sums_out.at[chunk, pl.ds(pl.multiple_of(target * CHUNK, CHUNK), CHUNK)],
-                  sums_in.at[chunk, off], s_send.at[chunk, off], s_recv.at[chunk, off])
-
-    def d_copy(chunk):
+    def d_copy(chunk, target):
         rows = pl.ds(pl.multiple_of(chunk * CHUNK, CHUNK), CHUNK)
-        return to(lax.rem(sec + n_sec - 1, n_sec), dp, mp, d_out.at[rows], d_in.at[rows],
-                  d_send.at[chunk], d_recv.at[chunk])
+        return to(ring(sec, n_sec - 1, n_sec), target, mp,
+                  d_out.at[chunk, target * CHUNK:(target + 1) * CHUNK], d_in.at[dp, rows],
+                  d_send.at[chunk, target], d_recv.at[chunk, dp])
+
+    def d_arrival(chunk, source):
+        rows = pl.ds(pl.multiple_of(chunk * CHUNK, CHUNK), CHUNK)
+        spot = d_in.at[source, rows]
+        return to(sec, dp, mp, spot, spot, d_send.at[chunk, 0], d_recv.at[chunk, source])
 
     def in_copy(off):
         return to(sec, dp, ring(mp, off, n_mp), in_slots.at[0], in_slots.at[off],
@@ -189,10 +198,10 @@
 
     @pl.when(sec == top)
     def _():
-        d_in[...] = cot[...]
+        d_own[...] = cot[...]
         g_own[...] = (cot[...].astype(jnp.float32) * slope[...]).astype(jnp.bfloat16)
 
-    pl.semaphore_wait(barrier, group - 1 + n_sec - 1)
+    pl.semaphore_wait(barrier, group - 1 + n_sec - 1 + 2 * (n_dp - 1))
 
     q_row = lax.broadcasted_iota(jnp.int32, total.shape, 0)
     r_lane = lax.broadcasted_iota(jnp.int32, total.shape, 1)
@@ -250,23 +259,28 @@
 
     def take(chunk):
         rows = step_rows(chunk)
-        d_copy(chunk).wait_recv()
-        g_own[rows, :] = (d_in[rows, :].astype(jnp.float32) * slope[rows, :]).astype(jnp.bfloat16)
+        delta = jnp.zeros((CHUNK, piece), jnp.float32)
+        for source in range(n_dp):
+            d_arrival(chunk, source).wait_recv()
+            delta = delta + d_in[source, rows, :].astype(jnp.float32)
+        delta = delta.astype(jnp.bfloat16)
+        d_own[rows, :] = delta
+        g_own[rows, :] = (delta.astype(jnp.float32) * slope[rows, :]).astype(jnp.bfloat16)
 
     def multiply(chunk):
         rows = step_rows(chunk)
         g_wait(chunk)
         for part in range(W_PARTS):
             cols = slice(part * w_rows, (part + 1) * w_rows)
-            sums_out[chunk, :, cols] = dot_t(w_here[cols, :], g_all[chunk]).T
-        for off in range(1, n_dp):
-            s_copy(chunk, off).start()
-        back = sums_out[chunk, pl.ds(pl.multiple_of(dp * CHUNK, CHUNK), CHUNK), :]
-        for off in range(1, n_dp):
-            s_copy(chunk, off).wait_recv()
-            back = back + sums_in[chunk, off]
-        d_out[rows, :] = (d_in[rows, :].astype(jnp.float32) + back).astype(jnp.bfloat16)
-        d_copy(chunk).start()
+            back = dot_t(w_here[cols, :], g_all[chunk]).T
+            delta = d_own[rows, cols].astype(jnp.float32)
+            for target in range(n_dp):
+                at = slice(target * CHUNK, (target + 1) * CHUNK)
+                d_out[chunk, at, cols] = (
+                    back[at] + jnp.where(dp == target, delta, 0.0)
+                ).astype(jnp.bfloat16)
+        for target in range(n_dp):
+            d_copy(chunk, target).start()
 
     def project(example):
         rows = pl.ds(pl.multiple_of(example * LEN, LEN), LEN)
@@ -391,9 +405,8 @@
         @pl.loop(0, chunks)
         def _(chunk):
             g_move(chunk, lambda copy: copy.wait_send())
-            for off in range(1, n_dp):
-                s_copy(chunk, off).wait_send()
-            d_copy(chunk).wait_send()
+            for target in range(n_dp):
+                d_copy(chunk, target).wait_send()
 
 
 def body(sizes, cotangent, saved_inputs, pre_acts, weights, proj_in, proj_out, query_panels, partners):
@@ -433,9 +446,8 @@
             pltpu.VMEM((tokens, piece), jnp.bfloat16),
             pltpu.VMEM((chunks, n_dp * CHUNK, w_cols), jnp.bfloat16),
             pltpu.VMEM((tokens, piece), jnp.bfloat16),
-            pltpu.VMEM((tokens, piece), jnp.bfloat16),
-            pltpu.VMEM((chunks, n_dp * CHUNK, piece), jnp.float32),
-            pltpu.VMEM((chunks, n_dp, CHUNK, piece), jnp.float32),
+            pltpu.VMEM((n_dp, tokens, piece), jnp.bfloat16),
+            pltpu.VMEM((chunks, n_dp * CHUNK, piece), jnp.bfloat16),
             pltpu.VMEM((tokens, piece), jnp.float32),
             pltpu.VMEM((n_mp, tokens // 2, 2 * rank), jnp.float32),
             pltpu.VMEM((n_mp, examples, LEN, 2 * rank), jnp.bfloat16),
@@ -451,7 +463,6 @@
             dma((7,)),
             dma((n_dp,)), dma((n_dp,)),
             dma((chunks, piece // unit, n_mp)), dma((chunks, w_cols // unit, n_dp)),
-            dma((chunks,)), dma((chunks,)),
             dma((chunks, n_dp)), dma((chunks, n_dp)),
             dma((n_mp,)), dma((n_mp,)),
             dma((examples, n_mp)), dma((examples, n_mp)),

time: 77.7 us -> 73.8 us (0.950)
  Pallas kernels: 74.2 us -> 70.3 us
    pallas_call x1, Pallas kernels: 74.2 us -> 70.3 us  [body(): pl.pallas_call(functools.partial(relay_kernel, sizes), out_shape=(jax.Sha...]
where the time goes in v5:
time: 73.8 us; the launch traced here: 73.5 us
  Pallas kernels  70.3 us (95%)
  local copies, waits for them, and re-layouts  2.59 us (4%)
    pallas_call x1, Pallas kernels, body(): pl.pallas_call(functools.partial(relay_kernel, sizes), out_shape=(jax.Sha...  70.3 us
    unnamed x2, local copies, waits for them, and re-layouts  2.59 us

profile of v5, /device:TPU:0, one launch (start us, length us, event | category | flops | bytes accessed | tf_op | source)
XLA Modules:
  0.0 73.5 jit_solution(5737517961934786258)
XLA Ops:
  0.6 70.3 %shard_map.95 = (f32[1,4,1024]{2,1,0:T(4,128)}, f32[4,2,4]{2,1,0:T(2,128)}) custom-call(bf16[128,1024]{1,0:T(8,128)(2,1)} %cot_hbm.1, bf16[1,128,1024]{2,1,0:T(8,128)(2,1)} %inputs_hbm.1, bf16[1,128,1024]{2,1,0:T(8,128)(2,1)} %pre_hbm.1, bf16[1,1024,2048]{2,1,0:T(8,128)(2,1)} %weights.1, bf16[1,64,1024]{2,1,0:T(8,128)(2,1)} %bitcast.2, ...), custom_call_target="tpu_custom_call" | custom-call | flops 1073741824 | bytes 4194304 | tf_op jit(solution)/shard_map/pallas_call | solution.py:430
  70.9 1.3 %copy.12 = f32[1,4,1024]{2,1,0:T(4,128)} copy(f32[1,4,1024]{2,1,0:T(4,128)} %get-tuple-element.4) | data formatting | bytes 32768
  72.2 1.3 %copy.13 = f32[4,2,4]{2,1,0:T(2,128)} copy(f32[4,2,4]{2,1,0:T(2,128)} %get-tuple-element.5) | data formatting | bytes 256

commit v6 on v5

--- a/solution.py
+++ b/solution.py
@@ -56,7 +56,7 @@
             (proj_out_hbm.at[0], proj_wide.at[pl.ds(0, proj_out_hbm.shape[1])]), (weights.at[0], w_here),
         ))
     ]
-    for copy in loads:
+    for copy in loads[:-1]:
         copy.start()
     load_pre, load_cot, load_inputs, load_in, load_queries, load_out, load_w = loads
     chunks = tokens // CHUNK
@@ -190,18 +190,19 @@
     def c_copy(section):
         return to(section, dp, mp, result, result, c_send.at[section], c_recv)
 
+    def set_slopes(rows):
+        value = pre[rows, :].astype(jnp.float32)
+        sigma = 1.0 / (1.0 + jnp.exp(-value))
+        slope[rows, :] = sigma * (1.0 + value * (1.0 - sigma))
+
     load_pre.wait()
-    slope_pre = pre[...].astype(jnp.float32)
-    sigma = 1.0 / (1.0 + jnp.exp(-slope_pre))
-    slope[...] = sigma * (1.0 + slope_pre * (1.0 - sigma))
     load_cot.wait()
-
-    @pl.when(sec == top)
+    load_w.start()
+    pl.semaphore_wait(barrier, group - 1 + n_sec - 1 + 2 * (n_dp - 1))
+
+    @pl.when(sec < top)
     def _():
-        d_own[...] = cot[...]
-        g_own[...] = (cot[...].astype(jnp.float32) * slope[...]).astype(jnp.bfloat16)
-
-    pl.semaphore_wait(barrier, group - 1 + n_sec - 1 + 2 * (n_dp - 1))
+        set_slopes(slice(0, tokens))
 
     q_row = lax.broadcasted_iota(jnp.int32, total.shape, 0)
     r_lane = lax.broadcasted_iota(jnp.int32, total.shape, 1)
@@ -256,6 +257,12 @@
 
     def step_rows(chunk):
         return pl.ds(pl.multiple_of(chunk * CHUNK, CHUNK), CHUNK)
+
+    def open_top(chunk):
+        rows = step_rows(chunk)
+        set_slopes(rows)
+        d_own[rows, :] = cot[rows, :]
+        g_own[rows, :] = (cot[rows, :].astype(jnp.float32) * slope[rows, :]).astype(jnp.bfloat16)
 
     def take(chunk):
         rows = step_rows(chunk)
@@ -308,14 +315,19 @@
     proj_wide[rank:, :] = jnp.zeros((proj_wide.shape[0] - rank, piece), jnp.bfloat16)
     load_out.wait()
     pl.when(sec < top)(prepare)
-    load_w.wait()
 
     @pl.when(sec > 0)
     def _():
         @pl.loop(0, chunks + 1)
         def _(step):
+            pl.when(step == 1)(load_w.wait)
+
             @pl.when(step < chunks)
             def _():
+                @pl.when(sec == top)
+                def _():
+                    open_top(step)
+
                 @pl.when(sec < top)
                 def _():
                     take(step)
@@ -338,6 +350,8 @@
 
     @pl.when(sec == 0)
     def _():
+        load_w.wait()
+
         @pl.loop(0, chunks)
         def _(step):
             take(step)
@@ -409,6 +423,17 @@
                 d_copy(chunk, target).wait_send()
 
 
+def hand_over_kernel(panels, table, panels_out, table_out, done):
+    copies = [
+        pltpu.make_async_copy(panels, panels_out, done.at[0]),
+        pltpu.make_async_copy(table, table_out, done.at[1]),
+    ]
+    for copy in copies:
+        copy.start()
+    for copy in copies:
+        copy.wait()
+
+
 def body(sizes, cotangent, saved_inputs, pre_acts, weights, proj_in, proj_out, query_panels, partners):
     n_sec, n_dp, n_mp = sizes
     tokens, piece = cotangent.shape
@@ -427,12 +452,13 @@
     dma = pltpu.SemaphoreType.DMA
     vmem = pl.BlockSpec(memory_space=pltpu.VMEM)
     hbm = pl.BlockSpec(memory_space=pltpu.HBM)
-    return pl.pallas_call(
+    results = (
+        jax.ShapeDtypeStruct((1, examples, panel), jnp.float32),
+        jax.ShapeDtypeStruct((n_dp * asked, rounds, examples), jnp.float32),
+    )
+    made = pl.pallas_call(
         functools.partial(relay_kernel, sizes),
-        out_shape=(
-            jax.ShapeDtypeStruct((1, examples, panel), jnp.float32),
-            jax.ShapeDtypeStruct((n_dp * asked, rounds, examples), jnp.float32),
-        ),
+        out_shape=results,
         in_specs=[hbm] * 7 + [pl.BlockSpec(memory_space=pltpu.SMEM)],
         out_specs=(vmem, vmem),
         scratch_shapes=[
@@ -478,6 +504,14 @@
         ),
     )(cotangent, saved_inputs, pre_acts, weights, jnp.swapaxes(proj_in, 1, 2),
       jnp.swapaxes(proj_out, 1, 2), query_panels, partners)
+    return pl.pallas_call(
+        hand_over_kernel,
+        out_shape=results,
+        in_specs=[hbm, hbm],
+        out_specs=(hbm, hbm),
+        scratch_shapes=[dma((2,))],
+        compiler_params=pltpu.CompilerParams(vmem_limit_bytes=64 * 1024 * 1024),
+    )(*made)
 
 
 def solution(mesh):

time: 73.8 us -> 72.4 us (0.981)
  local copies, waits for them, and re-layouts: 2.59 us -> 0 us
  Pallas kernels: 70.3 us -> 71.6 us
    unnamed x2 -> x0, local copies, waits for them, and re-layouts: 2.59 us -> none
    pallas_call x1 -> x2, Pallas kernels: 70.3 us -> 71.6 us  [the longest x1 69.9 us: body(): pl.pallas_call(functools.partial(relay_kernel, sizes), out_shape=results,...]
where the time goes in v6:
time: 72.4 us; the launch traced here: 72.3 us
  Pallas kernels  71.6 us (99%)
    pallas_call x1, Pallas kernels, body(): pl.pallas_call(functools.partial(relay_kernel, sizes), out_shape=results,...  69.9 us
    pallas_call x1, Pallas kernels, body(): pl.pallas_call(hand_over_kernel, out_shape=results, in_specs=[hbm, hbm],...  1.74 us

profile of v6, /device:TPU:0, one launch (start us, length us, event | category | flops | bytes accessed | tf_op | source)
XLA Modules:
  0.0 72.3 jit_solution(2308693945277214075)
XLA Ops:
  0.6 69.9 %shard_map.95 = (f32[1,4,1024]{2,1,0:T(4,128)}, f32[4,2,4]{2,1,0:T(2,128)}) custom-call(bf16[128,1024]{1,0:T(8,128)(2,1)} %cot_hbm.1, bf16[1,128,1024]{2,1,0:T(8,128)(2,1)} %inputs_hbm.1, bf16[1,128,1024]{2,1,0:T(8,128)(2,1)} %pre_hbm.1, bf16[1,1024,2048]{2,1,0:T(8,128)(2,1)} %weights.1, bf16[1,64,1024]{2,1,0:T(8,128)(2,1)} %bitcast.2, ...), custom_call_target="tpu_custom_call" | custom-call | flops 1073741824 | bytes 4194304 | tf_op jit(solution)/shard_map/pallas_call | solution.py:459
  70.5 1.7 %shard_map.96 = (f32[1,4,1024]{2,1,0:T(4,128)}, f32[4,2,4]{2,1,0:T(2,128)}) custom-call(f32[1,4,1024]{2,1,0:T(4,128)} %get-tuple-element.4.panels, f32[4,2,4]{2,1,0:T(2,128)} %get-tuple-element.5.table), custom_call_target="tpu_custom_call" | custom-call | tf_op jit(solution)/shard_map/pallas_call | solution.py:507

commit v7 on v6

--- a/solution.py
+++ b/solution.py
@@ -11,6 +11,7 @@
 LEN = 32
 CHUNK = 16
 W_PARTS = 4
+D_PARTS = 2
 MESH = pl.DeviceIdType.MESH
 
 
@@ -160,16 +161,21 @@
                 else:
                     pl.when(source != mp)(arrival.wait_recv)
 
-    def d_copy(chunk, target):
+    d_width = piece // D_PARTS
+
+    def d_copy(chunk, part, target):
         rows = pl.ds(pl.multiple_of(chunk * CHUNK, CHUNK), CHUNK)
+        cols = slice(part * d_width, (part + 1) * d_width)
         return to(ring(sec, n_sec - 1, n_sec), target, mp,
-                  d_out.at[chunk, target * CHUNK:(target + 1) * CHUNK], d_in.at[dp, rows],
-                  d_send.at[chunk, target], d_recv.at[chunk, dp])
-
-    def d_arrival(chunk, source):
+                  d_out.at[chunk, target * CHUNK:(target + 1) * CHUNK, cols],
+                  d_in.at[dp, rows, cols],
+                  d_send.at[chunk, part, target], d_recv.at[chunk, part, dp])
+
+    def d_arrival(chunk, part, source):
         rows = pl.ds(pl.multiple_of(chunk * CHUNK, CHUNK), CHUNK)
-        spot = d_in.at[source, rows]
-        return to(sec, dp, mp, spot, spot, d_send.at[chunk, 0], d_recv.at[chunk, source])
+        spot = d_in.at[source, rows, part * d_width:(part + 1) * d_width]
+        return to(sec, dp, mp, spot, spot, d_send.at[chunk, part, 0],
+                  d_recv.at[chunk, part, source])
 
     def in_copy(off):
         return to(sec, dp, ring(mp, off, n_mp), in_slots.at[0], in_slots.at[off],
@@ -266,13 +272,17 @@
 
     def take(chunk):
         rows = step_rows(chunk)
-        delta = jnp.zeros((CHUNK, piece), jnp.float32)
-        for source in range(n_dp):
-            d_arrival(chunk, source).wait_recv()
-            delta = delta + d_in[source, rows, :].astype(jnp.float32)
-        delta = delta.astype(jnp.bfloat16)
-        d_own[rows, :] = delta
-        g_own[rows, :] = (delta.astype(jnp.float32) * slope[rows, :]).astype(jnp.bfloat16)
+        for part in range(D_PARTS):
+            cols = slice(part * d_width, (part + 1) * d_width)
+            delta = jnp.zeros((CHUNK, d_width), jnp.float32)
+            for source in range(n_dp):
+                d_arrival(chunk, part, source).wait_recv()
+                delta = delta + d_in[source, rows, cols].astype(jnp.float32)
+            delta = delta.astype(jnp.bfloat16)
+            d_own[rows, cols] = delta
+            g_own[rows, cols] = (
+                delta.astype(jnp.float32) * slope[rows, cols]
+            ).astype(jnp.bfloat16)
 
     def multiply(chunk):
         rows = step_rows(chunk)
@@ -286,8 +296,9 @@
                 d_out[chunk, at, cols] = (
                     back[at] + jnp.where(dp == target, delta, 0.0)
                 ).astype(jnp.bfloat16)
-        for target in range(n_dp):
-            d_copy(chunk, target).start()
+            if (part + 1) % (W_PARTS // D_PARTS) == 0:
+                for target in range(n_dp):
+                    d_copy(chunk, part // (W_PARTS // D_PARTS), target).start()
 
     def project(example):
         rows = pl.ds(pl.multiple_of(example * LEN, LEN), LEN)
@@ -419,8 +430,9 @@
         @pl.loop(0, chunks)
         def _(chunk):
             g_move(chunk, lambda copy: copy.wait_send())
-            for target in range(n_dp):
-                d_copy(chunk, target).wait_send()
+            for part in range(D_PARTS):
+                for target in range(n_dp):
+                    d_copy(chunk, part, target).wait_send()
 
 
 def hand_over_kernel(panels, table, panels_out, table_out, done):
@@ -489,7 +501,7 @@
             dma((7,)),
             dma((n_dp,)), dma((n_dp,)),
             dma((chunks, piece // unit, n_mp)), dma((chunks, w_cols // unit, n_dp)),
-            dma((chunks, n_dp)), dma((chunks, n_dp)),
+            dma((chunks, D_PARTS, n_dp)), dma((chunks, D_PARTS, n_dp)),
             dma((n_mp,)), dma((n_mp,)),
             dma((examples, n_mp)), dma((examples, n_mp)),
             dma, dma((n_sec,)),

time: 72.4 us -> 72.6 us (level)
  no operation moved by 1% of the time
where the time goes in v7:
time: 72.6 us; the launch traced here: 72.5 us
  Pallas kernels  71.8 us (99%)
    pallas_call x1, Pallas kernels, body(): pl.pallas_call(functools.partial(relay_kernel, sizes), out_shape=results,...  70.1 us
    pallas_call x1, Pallas kernels, body(): pl.pallas_call(hand_over_kernel, out_shape=results, in_specs=[hbm, hbm],...  1.74 us

profile of v7, /device:TPU:0, one launch (start us, length us, event | category | flops | bytes accessed | tf_op | source)
XLA Modules:
  0.0 72.5 jit_solution(94885695299082682)
XLA Ops:
  0.6 70.1 %shard_map.95 = (f32[1,4,1024]{2,1,0:T(4,128)}, f32[4,2,4]{2,1,0:T(2,128)}) custom-call(bf16[128,1024]{1,0:T(8,128)(2,1)} %cot_hbm.1, bf16[1,128,1024]{2,1,0:T(8,128)(2,1)} %inputs_hbm.1, bf16[1,128,1024]{2,1,0:T(8,128)(2,1)} %pre_hbm.1, bf16[1,1024,2048]{2,1,0:T(8,128)(2,1)} %weights.1, bf16[1,64,1024]{2,1,0:T(8,128)(2,1)} %bitcast.2, ...), custom_call_target="tpu_custom_call" | custom-call | flops 1073741824 | bytes 4194304 | tf_op jit(solution)/shard_map/pallas_call | solution.py:471
  70.7 1.7 %shard_map.96 = (f32[1,4,1024]{2,1,0:T(4,128)}, f32[4,2,4]{2,1,0:T(2,128)}) custom-call(f32[1,4,1024]{2,1,0:T(4,128)} %get-tuple-element.4.panels, f32[4,2,4]{2,1,0:T(2,128)} %get-tuple-element.5.table), custom_call_target="tpu_custom_call" | custom-call | tf_op jit(solution)/shard_map/pallas_call | solution.py:519

commit v8 on v6

--- a/solution.py
+++ b/solution.py
@@ -128,7 +128,7 @@
     def g_move(chunk, act):
         for sub in range(piece // unit):
             target, _ = g_target(sub)
-            for off in range(1, n_mp):
+            for off in sorted(range(1, n_mp), key=lambda off: abs(2 * off - n_mp)):
                 act(g_copy(chunk, sub, off))
 
             @pl.when(target != dp)

time: 72.4 us -> 73.9 us (1.021)
  Pallas kernels: 71.6 us -> 73.1 us
    pallas_call x1, Pallas kernels: 69.9 us -> 71.3 us  [body(): pl.pallas_call(functools.partial(relay_kernel, sizes), out_shape=results,...]
where the time goes in v8:
time: 73.9 us; the launch traced here: 73.7 us
  Pallas kernels  73.1 us (99%)
    pallas_call x1, Pallas kernels, body(): pl.pallas_call(functools.partial(relay_kernel, sizes), out_shape=results,...  71.3 us
    pallas_call x1, Pallas kernels, body(): pl.pallas_call(hand_over_kernel, out_shape=results, in_specs=[hbm, hbm],...  1.74 us

profile of v8, /device:TPU:0, one launch (start us, length us, event | category | flops | bytes accessed | tf_op | source)
XLA Modules:
  0.0 73.7 jit_solution(873789296658164684)
XLA Ops:
  0.6 71.3 %shard_map.95 = (f32[1,4,1024]{2,1,0:T(4,128)}, f32[4,2,4]{2,1,0:T(2,128)}) custom-call(bf16[128,1024]{1,0:T(8,128)(2,1)} %cot_hbm.1, bf16[1,128,1024]{2,1,0:T(8,128)(2,1)} %inputs_hbm.1, bf16[1,128,1024]{2,1,0:T(8,128)(2,1)} %pre_hbm.1, bf16[1,1024,2048]{2,1,0:T(8,128)(2,1)} %weights.1, bf16[1,64,1024]{2,1,0:T(8,128)(2,1)} %bitcast.2, ...), custom_call_target="tpu_custom_call" | custom-call | flops 1073741824 | bytes 4194304 | tf_op jit(solution)/shard_map/pallas_call | solution.py:459
  72.0 1.7 %shard_map.96 = (f32[1,4,1024]{2,1,0:T(4,128)}, f32[4,2,4]{2,1,0:T(2,128)}) custom-call(f32[1,4,1024]{2,1,0:T(4,128)} %get-tuple-element.4.panels, f32[4,2,4]{2,1,0:T(2,128)} %get-tuple-element.5.table), custom_call_target="tpu_custom_call" | custom-call | tf_op jit(solution)/shard_map/pallas_call | solution.py:507
